TPU v7x, 512 devices: a whole 4x8x8 slice. The times are simulated.
512 devices in a mesh: sec: 32 (over x, y), head: 16 (over z, core).
Axes of the slice: x: 4, y: 8, z: 8, core: 2. Of those that a mesh axis runs over, the one named last changes fastest.
Arguments:
- tokens: bfloat16 [32768, 2048], P('sec', 'head'), may hold values from -6 to 6
- fresh_tokens: bfloat16 [1024, 2048], P(None, 'head'), may hold values from -6 to 6
- route_rows: int32 [32, 4, 128], P('sec'), may hold values from 0 to 255, as said below
- block_list: int32 [32, 4, 16], P('sec'), may hold values from 0 to 31, all different within a row
- norm_gain: float32 [32, 2048], P('sec'), may hold values from 0.25 to 1.75
- route_weight: bfloat16 [32, 2048], P('sec'), may hold values from -0.125 to 0.125
- w_query: bfloat16 [32, 2048, 2048], P('sec', None, 'head'), may hold values from -0.125 to 0.125
- w_key: bfloat16 [32, 2048, 2048], P('sec', None, 'head'), may hold values from -0.26367188 to 0.26367188
- w_value: bfloat16 [32, 2048, 2048], P('sec', None, 'head'), may hold values from -0.125 to 0.125
- w_out: bfloat16 [32, 2048, 2048], P('sec', None, 'head'), may hold values from -0.52734375 to 0.52734375
- cache_keys: bfloat16 [32, 4096, 2048], P('sec', None, 'head'), may hold values from -2400 to 2400
- cache_values: bfloat16 [32, 4096, 2048], P('sec', None, 'head'), may hold values from -6 to 6
Outputs:
- next_input: bfloat16 [32768, 2048], P('sec', 'head')
Inputs may be any that keep to these rules, and one draw needn't show every extreme that they name: `route_rows`: within one section and group the 128 entries are distinct row numbers of the group. `block_list`: each section's group names 16 distinct blocks.
All inputs are finite; a program needn't handle non-finite values.
Results may differ from a plain program's by a relative error of at most 0.017.
Values may be sent and summed in bfloat16 or wider, within the bound.
A program may use at most 64 MiB of HBM per device.

v0:
```python
import math
import jax
import jax.numpy as jnp
from jax import lax
from jax.sharding import Mesh
from jax.sharding import PartitionSpec as P

HEAD_DIM = 64
BLOCK = 128
HEAD = ("head_0", "head_1")


def gathered_by_axis(shard, axes, dim):
    if not axes:
        return shard
    nearer = lax.all_gather(shard, axes[-1], axis=dim, tiled=True)
    return gathered_by_axis(nearer, axes[:-1], dim)


def shifted_2(shard, axis, by):
    length = lax.axis_size(axis)
    pairs = [(i, i + by) for i in range(length) if 0 <= i + by < length]
    return lax.ppermute(shard, axis, pairs)


def attend_local(queries, key_rows, value_rows, row_index, cache_k, cache_v, picks):
    row_count, head_count, head_width = queries.shape
    group_count = picks.shape[0]
    score_scale = 1.0 / math.sqrt(head_width)
    chosen_keys = cache_k.reshape(-1, BLOCK, head_count, head_width)[picks].reshape(
        group_count, -1, head_count, head_width
    )
    chosen_values = cache_v.reshape(-1, BLOCK, head_count, head_width)[picks].reshape(
        group_count, -1, head_count, head_width
    )
    query_groups = queries.reshape(group_count, -1, head_count, head_width)
    cache_scores = (
        jnp.einsum("crhd,ckhd->chrk", query_groups, chosen_keys, preferred_element_type=jnp.float32)
        * score_scale
    )
    local_scores = (
        jnp.einsum("qhd,khd->hqk", queries, key_rows, preferred_element_type=jnp.float32)
        * score_scale
    )
    visible = row_index[None, :] <= row_index[:, None]
    local_scores = jnp.where(visible[None], local_scores, -jnp.inf)
    cache_max = jnp.transpose(jnp.max(cache_scores, axis=-1), (1, 0, 2)).reshape(
        head_count, row_count
    )
    row_max = jnp.maximum(cache_max, jnp.max(local_scores, axis=-1))
    group_max = jnp.transpose(row_max.reshape(head_count, group_count, -1), (1, 0, 2))
    cache_weights = jnp.exp(cache_scores - group_max[..., None])
    local_weights = jnp.exp(local_scores - row_max[..., None])
    cache_sum = jnp.transpose(jnp.sum(cache_weights, axis=-1), (1, 0, 2)).reshape(
        head_count, row_count
    )
    denom_sum = cache_sum + jnp.sum(local_weights, axis=-1)
    from_cache = jnp.einsum(
        "chrk,ckhd->crhd",
        cache_weights.astype(jnp.bfloat16),
        chosen_values,
        preferred_element_type=jnp.float32,
    ).reshape(row_count, head_count, head_width)
    from_local = jnp.einsum(
        "hqk,khd->qhd",
        local_weights.astype(jnp.bfloat16),
        value_rows,
        preferred_element_type=jnp.float32,
    )
    attended = (from_cache + from_local) / jnp.transpose(denom_sum)[:, :, None]
    return attended.astype(jnp.bfloat16).reshape(row_count, head_count * head_width)


def body(
    tokens,
    fresh_tokens,
    route_rows,
    block_list,
    norm_gain,
    route_weight,
    w_query,
    w_key,
    w_value,
    w_out,
    cache_keys,
    cache_values,
):
    group_count = route_rows.shape[1]
    group_rows = tokens.shape[0] // group_count
    row_index = (
        route_rows[0] + group_rows * jnp.arange(group_count, dtype=jnp.int32)[:, None]
    ).reshape(-1)
    own_rows = jnp.take(tokens, row_index, axis=0)
    picked_rows = gathered_by_axis(own_rows, HEAD, 1)
    picked = picked_rows.astype(jnp.float32)
    mean_square = jnp.mean(picked * picked, axis=-1, keepdims=True)
    normed = (picked * lax.rsqrt(mean_square + 1e-05) * norm_gain[0][None, :]).astype(jnp.bfloat16)
    gate_value = jax.nn.sigmoid(
        jnp.dot(normed, route_weight[0], preferred_element_type=jnp.float32)
    )
    local_heads = w_query.shape[2] // HEAD_DIM
    queries = (
        jnp.dot(normed, w_query[0], preferred_element_type=jnp.float32)
        .astype(jnp.bfloat16)
        .reshape(-1, local_heads, HEAD_DIM)
    )
    key_rows = (
        jnp.dot(normed, w_key[0], preferred_element_type=jnp.float32)
        .astype(jnp.bfloat16)
        .reshape(-1, local_heads, HEAD_DIM)
    )
    value_rows = (
        jnp.dot(normed, w_value[0], preferred_element_type=jnp.float32)
        .astype(jnp.bfloat16)
        .reshape(-1, local_heads, HEAD_DIM)
    )
    attended = attend_local(
        queries, key_rows, value_rows, row_index, cache_keys[0], cache_values[0], block_list[0]
    )
    output_rows = w_out[0]
    branch = jnp.dot(
        lax.all_gather(attended, HEAD, axis=1, tiled=True),
        output_rows,
        preferred_element_type=jnp.float32,
    )
    own_columns = jnp.take(tokens, row_index, axis=0).astype(jnp.float32)
    updated = (own_columns + gate_value[:, None] * branch).astype(jnp.bfloat16)
    result = tokens.at[row_index].set(updated)
    shifted = shifted_2(result, "sec", 1)
    return jnp.where(lax.axis_index("sec") == 0, fresh_tokens, shifted)


def solution(mesh):
    torus = Mesh(mesh.devices.reshape(mesh.shape["sec"], 8, 2), ("sec", "head_0", "head_1"))
    in_specs = (
        P("sec", HEAD),
        P(None, HEAD),
        P("sec", None, None),
        P("sec", None, None),
        P("sec", None),
        P("sec", None),
        P("sec", None, HEAD),
        P("sec", None, HEAD),
        P("sec", None, HEAD),
        P("sec", None, HEAD),
        P("sec", None, HEAD),
        P("sec", None, HEAD),
    )
    out_specs = P("sec", HEAD)
    return jax.shard_map(body, mesh=torus, in_specs=in_specs, out_specs=out_specs, check_vma=False)
```

profile of v0, /device:TPU:2, one launch (start us, length us, event | category | flops | bytes accessed | tf_op | source)
XLA Modules:
  0.0 152.1 jit_solution(10076083262525095151)
XLA Ops:
  6.5 0.0 copy-start
  6.5 0.0 copy-start.10
  6.5 0.0 copy-start.4
  6.5 0.0 all-gather.3.cloned.1.call-start
  6.5 1.1 copy.65
  7.6 0.8 compare_and_fusion
  8.4 1.3 gather_fusion.2
  9.7 0.1 broadcast_select_fusion.1
  9.9 2.1 %all_gather.9 = bf16[512,256]{1,0:T(8,128)(2,1)} all-gather(bf16[512,128]{1,0:T(8,128)(2,1)S(1)} %broadcast_select_fusion.1), channel_id=1, replica_groups=mesh['sec'=32,'head_0'=8,'head_1'=2] {'head_1'}, dimensions={1}, use_global_device_ids=true | all-gather | bytes 393216 | tf_op jit(solution)/shard_map/all_gather | solution.py:16
  12.0 0.0 all-gather.3.cloned.1.call-update
  12.0 0.0 all-gather.5.cloned.1.call-start
  12.1 0.0 copy-done.10
  12.1 0.1 reshape.179
  12.2 0.0 copy-done.4
  12.2 1.8 %reshape.212 = bf16[32,128,2,64]{3,2,1,0:T(2,128)(2,1)} reshape(bf16[1,4096,128]{2,1,0:T(8,128)(2,1)S(1)} %copy-done.4) | data formatting | bytes 2097152 | tf_op jit(solution)/shard_map/reshape;squeeze | solution.py:30
  14.0 5.0 %copy.37 = bf16[32,128,2,64]{1,3,2,0:T(8,128)(2,1)S(1)} copy(bf16[32,128,2,64]{3,2,1,0:T(2,128)(2,1)} %reshape.212) | data formatting | bytes 2097152 | tf_op jit(solution)/shard_map/reshape;squeeze | solution.py:30
  19.1 2.1 %gather_fusion.1 = bf16[64,128,2,64]{1,3,2,0:T(8,128)(2,1)} fusion(bf16[32,128,2,64]{1,3,2,0:T(8,128)(2,1)S(1)} %copy.37, s32[1024]{0:T(1024)S(1)} %pad_clamp_fusion), kind=kCustom, calls=%fused_computation.2 | custom fusion | bytes 4194560 | tf_op jit(solution)/shard_map/gather | solution.py:30
  21.2 2.9 %copy.38 = bf16[64,128,2,64]{1,0,3,2:T(8,128)(2,1)S(1)} copy(bf16[64,128,2,64]{1,3,2,0:T(8,128)(2,1)} %gather_fusion.1) | data formatting | bytes 4194304 | tf_op jit(solution)/shard_map/gather | solution.py:30
  24.1 2.0 %reshape.161 = bf16[4,2048,2,64]{1,0,3,2:T(4,128)(2,1)} reshape(bf16[64,128,2,64]{1,0,3,2:T(8,128)(2,1)S(1)} %copy.38) | data formatting | bytes 4194304 | tf_op jit(solution)/shard_map/reshape | solution.py:30
  26.2 5.0 %reshape.211 = bf16[32,128,2,64]{3,2,1,0:T(2,128)(2,1)} reshape(bf16[1,4096,128]{2,1,0:T(8,128)(2,1)} %param.25) | data formatting | bytes 2097152 | tf_op jit(solution)/shard_map/reshape;squeeze | solution.py:33
  31.2 5.1 %copy.34 = bf16[32,128,2,64]{1,3,2,0:T(8,128)(2,1)S(1)} copy(bf16[32,128,2,64]{3,2,1,0:T(2,128)(2,1)} %reshape.211) | data formatting | bytes 2097152 | tf_op jit(solution)/shard_map/reshape;squeeze | solution.py:33
  36.2 2.1 %gather_fusion = bf16[64,128,2,64]{1,3,2,0:T(8,128)(2,1)} fusion(bf16[32,128,2,64]{1,3,2,0:T(8,128)(2,1)S(1)} %copy.34, s32[1024]{0:T(1024)S(1)} %pad_clamp_fusion), kind=kCustom, calls=%fused_computation.1 | custom fusion | bytes 4194560 | tf_op jit(solution)/shard_map/gather | solution.py:33
  38.4 3.0 %copy.35 = bf16[64,128,2,64]{1,0,3,2:T(8,128)(2,1)S(1)} copy(bf16[64,128,2,64]{1,3,2,0:T(8,128)(2,1)} %gather_fusion) | data formatting | bytes 4194304 | tf_op jit(solution)/shard_map/gather | solution.py:33
  41.4 2.1 %reshape.160 = bf16[4,2048,2,64]{1,0,3,2:T(4,128)(2,1)} reshape(bf16[64,128,2,64]{1,0,3,2:T(8,128)(2,1)S(1)} %copy.35) | data formatting | bytes 4194304 | tf_op jit(solution)/shard_map/reshape | solution.py:33
  43.5 0.0 copy-start.7
  43.5 0.2 broadcast_compare_fusion
  43.7 23.5 %all-gather.3.cloned.1.call-done = bf16[512,2048]{1,0:T(8,128)(2,1)} async-done(((bf16[512,256]{1,0:T(8,128)(2,1)}), bf16[512,2048]{1,0:T(8,128)(2,1)}) %all-gather.3.cloned.1.call-update) | async-done | bytes 2097168 | tf_op jit(solution)/shard_map/all_gather | solution.py:16
  67.2 0.0 copy-start.3
  67.2 2.2 %fusion.2 = f32[512]{0:T(512)S(1)} fusion(bf16[512,2048]{1,0:T(8,128)(2,1)} %all-gather.3.cloned.1.call-done), kind=kLoop, calls=%fused_computation.10 | loop fusion | flops 3145216 | bytes 2099200 | tf_op jit(solution)/shard_map/reduce_sum | solution.py:96
  69.5 0.0 copy-done.7
  69.5 0.0 copy-done.3
  69.5 0.5 fusion.4
  70.0 0.0 copy-done
  70.0 0.8 convolution_convert_fusion.2
  70.9 0.0 copy-start.2
  70.9 2.0 %convolution_convert_fusion.1 = bf16[512,128]{0,1:T(8,128)(2,1)S(1)} fusion(bf16[512,2048]{1,0:T(8,128)(2,1)S(1)} %fusion.4, bf16[1,2048,128]{2,1,0:T(8,128)(2,1)} %param.21), kind=kOutput, calls=%fused_computation.32 | convolution fusion | flops 268500992 | bytes 2752512 | tf_op jit(solution)/shard_map/dot_general | solution.py:108
  72.9 0.0 copy-done.2
  72.9 3.4 %multiply_reduce_fusion = (f32[4,2,128]{2,1,0:T(2,128)S(1)}, f32[4,2,128,2048]{3,2,1,0:T(8,128)S(1)}) fusion(bf16[4,2048,2,64]{1,0,3,2:T(4,128)(2,1)S(1)} %copy-done.2, bf16[4,128,2,64]{1,0,3,2:T(4,128)(2,1)S(1)} %reshape_reshape.3), kind=kOutput, calls=%fused_computation.5 | convolution fusion | flops 272628736 | bytes 10620928 | tf_op jit(solution)/shard_map/crhd,ckhd->chrk/dot_general | solution.py:38
  76.3 0.0 copy-start.5
  76.3 0.6 fusion.12
  77.0 0.4 copy-done.5
  77.4 0.8 convolution_convert_fusion
  78.2 0.0 copy-start.1
  78.2 1.6 %fusion = f32[4,2,128]{2,1,0:T(2,128)S(1)} fusion(f32[4,2,128,2048]{3,2,1,0:T(8,128)S(1)} %get-tuple-element.11, f32[4,2,128]{2,1,0:T(2,128)S(1)} %fusion.37), kind=kLoop, calls=%fused_computation.6 | loop fusion | flops 6290432 | bytes 8396800 | tf_op jit(solution)/shard_map/reduce_sum | solution.py:54
  79.8 0.0 copy-done.1
  79.9 3.6 %fusion.18 = f32[4,2,8,8,128]{4,3,2,1,0:T(8,128)S(1)} fusion(f32[4,2,128,2048]{3,2,1,0:T(8,128)S(1)} %get-tuple-element.11, f32[4,2,128]{2,1,0:T(2,128)S(1)} %fusion.37, bf16[4,2048,2,64]{1,0,3,2:T(4,128)(2,1)S(1)} %copy-done.1), kind=kOutput, calls=%fused_computation.29 | convolution fusion | flops 274726912 | bytes 10752000 | tf_op jit(solution)/shard_map/chrk,ckhd->crhd/dot_general | solution.py:58
  83.5 0.5 fusion.13
  84.0 0.0 copy-start.9
  84.0 0.0 copy-start.8
  84.0 1.4 fusion.24
  85.4 0.0 all-gather.5.cloned.1.call-update
  85.4 0.1 add.84
  85.5 0.0 copy-done.9
  85.5 0.0 copy-done.8
  85.5 0.6 fusion.34
  86.2 0.0 copy-start.6
  86.2 41.6 %all-gather.5.cloned.1.call-done = bf16[512,2048]{0,1:T(8,128)(2,1)} async-done(((bf16[512,128]{0,1:T(8,128)(2,1)}), bf16[512,2048]{0,1:T(8,128)(2,1)}) %all-gather.5.cloned.1.call-update) | async-done | bytes 2097168 | tf_op jit(solution)/shard_map/all_gather | solution.py:122
  127.7 2.4 %fusion.23 = bf16[512,128]{1,0:T(8,128)(2,1)S(1)} fusion(bf16[512,2048]{0,1:T(8,128)(2,1)} %all-gather.5.cloned.1.call-done, bf16[1,2048,128]{2,1,0:T(8,128)(2,1)} %param.23, bf16[512,128]{1,0:T(8,128)(2,1)S(1)} %broadcast_select_fusion.1, f32[512]{0:T(512)S(1)} %add_divide_fusion), kind=kOutput, calls=%fused_computation.30 | convolution fusion | flops 268697600 | bytes 2885632 | tf_op jit(solution)/shard_map/dot_general | solution.py:121
  130.2 1.9 %scatter_fusion = bf16[1024,128]{1,0:T(8,128)(2,1)S(1)} fusion(bf16[1024,128]{1,0:T(8,128)(2,1)S(1)} %copy.65, s32[512]{0:T(512)S(1)} %bitcast.90, bf16[512,128]{1,0:T(8,128)(2,1)S(1)} %fusion.23), kind=kCustom, calls=%fused_computation.3 | custom fusion | bytes 395264 | tf_op jit(solution)/shard_map/scatter | solution.py:128
  132.1 3.4 %collective-permute-start = (bf16[1024,128]{1,0:T(8,128)(2,1)S(1)}, bf16[1024,128]{1,0:T(8,128)(2,1)S(1)}, u32[]{:S(2)}, u32[]{:S(2)}) collective-permute-start(bf16[1024,128]{1,0:T(8,128)(2,1)S(1)} %scatter_fusion), channel_id=1, source_target_pairs={{0,16},{16,32},{32,48},{48,64},{64,80},{80,96},{96,112},{112,128},... | collective-permute-start | bytes 786440 | tf_op jit(solution)/shard_map/ppermute | solution.py:23
  135.5 9.1 %collective-permute-done = bf16[1024,128]{1,0:T(8,128)(2,1)S(1)} collective-permute-done((bf16[1024,128]{1,0:T(8,128)(2,1)S(1)}, bf16[1024,128]{1,0:T(8,128)(2,1)S(1)}, u32[]{:S(2)}, u32[]{:S(2)}) %collective-permute-start) | collective-permute-done | bytes 262176 | tf_op jit(solution)/shard_map/ppermute | solution.py:23
  144.6 0.0 copy-done.6
  144.6 0.7 broadcast_select_fusion
  (12 shorter events, 0.1 us)
Async XLA Ops:
  6.5 63.5 %copy-start = (bf16[1,2048,128]{2,1,0:T(8,128)(2,1)S(1)}, bf16[1,2048,128]{2,1,0:T(8,128)(2,1)}, u32[]{:S(2)}) copy-start(bf16[1,2048,128]{2,1,0:T(8,128)(2,1)} %param.20) | copy-start | bytes 1572868
  6.5 5.5 %copy-start.10 = (s32[1,4,16]{2,1,0:T(4,128)S(1)}, s32[1,4,16]{2,1,0:T(4,128)}, u32[]{:S(2)}) copy-start(s32[1,4,16]{2,1,0:T(4,128)} %param.17) | copy-start | bytes 772
  6.5 5.7 %copy-start.4 = (bf16[1,4096,128]{2,1,0:T(8,128)(2,1)S(1)}, bf16[1,4096,128]{2,1,0:T(8,128)(2,1)}, u32[]{:S(2)}) copy-start(bf16[1,4096,128]{2,1,0:T(8,128)(2,1)} %param.24) | copy-start | bytes 3145732
  6.5 60.7 %all-gather.3.cloned.1.call-start = ((), (), s32[]{:S(2)}) async-start(), calls=%async_computation | async-start | bytes 2359296 | tf_op jit(solution)/shard_map/all_gather | solution.py:16
  12.0 115.7 %all-gather.5.cloned.1.call-start = ((), (), s32[]{:S(2)}) async-start(), calls=%async_computation.1 | async-start | bytes 2228224 | tf_op jit(solution)/shard_map/all_gather | solution.py:122
  43.5 26.0 %copy-start.7 = (f32[1,2048]{1,0:T(1,128)S(1)}, f32[1,2048]{1,0:T(1,128)}, u32[]{:S(2)}) copy-start(f32[1,2048]{1,0:T(1,128)} %param.18) | copy-start | bytes 24580
  67.2 2.2 %copy-start.3 = (bf16[512,2048]{1,0:T(8,128)(2,1)S(1)}, bf16[512,2048]{1,0:T(8,128)(2,1)}, u32[]{:S(2)}) copy-start(bf16[512,2048]{1,0:T(8,128)(2,1)} %all-gather.3.cloned.1.call-done) | copy-start | bytes 6291460
  70.9 2.0 %copy-start.2 = (bf16[4,2048,2,64]{1,0,3,2:T(4,128)(2,1)S(1)}, bf16[4,2048,2,64]{1,0,3,2:T(4,128)(2,1)}, u32[]{:S(2)}) copy-start(bf16[4,2048,2,64]{1,0,3,2:T(4,128)(2,1)} %reshape.161) | copy-start | bytes 6291460
  76.3 1.0 copy-start.5
  78.2 1.7 %copy-start.1 = (bf16[4,2048,2,64]{1,0,3,2:T(4,128)(2,1)S(1)}, bf16[4,2048,2,64]{1,0,3,2:T(4,128)(2,1)}, u32[]{:S(2)}) copy-start(bf16[4,2048,2,64]{1,0,3,2:T(4,128)(2,1)} %reshape.160) | copy-start | bytes 6291460
  84.0 1.5 copy-start.9
  84.0 1.5 copy-start.8
  86.2 58.4 %copy-start.6 = (bf16[1024,128]{1,0:T(8,128)(2,1)S(1)}, bf16[1024,128]{1,0:T(8,128)(2,1)}, u32[]{:S(2)}) copy-start(bf16[1024,128]{1,0:T(8,128)(2,1)} %param.15) | copy-start | bytes 786436
  132.1 12.5 %collective-permute-start = (bf16[1024,128]{1,0:T(8,128)(2,1)S(1)}, bf16[1024,128]{1,0:T(8,128)(2,1)S(1)}, u32[]{:S(2)}, u32[]{:S(2)}) collective-permute-start(bf16[1024,128]{1,0:T(8,128)(2,1)S(1)} %scatter_fusion), channel_id=1, source_target_pairs={{0,16},{16,32},{32,48},{48,64},{64,80},{80,96},{96,112},{112,128},... | collective-permute-start | bytes 786440 | tf_op jit(solution)/shard_map/ppermute | solution.py:23
Sparse Core Ops, SparseCore 0:
  12.2 55.0 all-gather.2
  85.5 42.1 all-gather.4
where the time goes:
time: 153 us; the launch traced here: 152 us
  waiting for transfers between devices  74.2 us (48%)
  local copies, waits for them, and re-layouts  36.2 us (24%)
  matrix products  15.7 us (10%)
  between operations  13.7 us (9%)
  other arithmetic  6.82 us (4%)
  starting transfers between devices  3.44 us (2%)
  blocking collectives  2.13 us (1%)
    all_gather x1, waiting for transfers between devices, body(): lax.all_gather(attended, HEAD, axis=1, tiled=True)  41.6 us
    all_gather x1, waiting for transfers between devices, gathered_by_axis(): nearer = lax.all_gather(shard, axes[-1], axis=dim, tiled=True)  23.5 us
    another operation x2, local copies, waits for them, and re-layouts, attend_local(): cache_v.reshape(-1, BLOCK, head_count, head_width)[picks]  10 us
    ppermute x1, waiting for transfers between devices, shifted_2(): return lax.ppermute(shard, axis, pairs)  9.06 us
    another operation x2, local copies, waits for them, and re-layouts, attend_local(): cache_k.reshape(-1, BLOCK, head_count, head_width)[picks]  6.87 us
    gather x2, local copies, waits for them, and re-layouts, attend_local(): cache_v.reshape(-1, BLOCK, head_count, head_width)[picks]  5.13 us
    gather x2, local copies, waits for them, and re-layouts, attend_local(): cache_k.reshape(-1, BLOCK, head_count, head_width)[picks]  5.07 us
    dot_general x1, matrix products, attend_local(): jnp.einsum('chrk,ckhd->crhd', cache_weights.astype(jnp.bfloat16), chosen_...  3.63 us
  transfers between devices with their start and end apart: 3, of which 3 were waited for; matrix products, arithmetic and copies ran while one was open for 21% of the time, Pallas kernels for 0%

commit v1 on v0

--- a/solution.py
+++ b/solution.py
@@ -8,6 +8,13 @@
 HEAD_DIM = 64
 BLOCK = 128
 HEAD = ("head_0", "head_1")
+
+
+def _return_all_floor(arr_in, axis_no):
+    e_now = jax.lax.psum(1, HEAD)
+    step_out = jnp.stack([arr_in] * e_now)
+    plain = jax.lax.all_to_all(step_out, HEAD, 0, 0)
+    return jnp.concatenate(plain, axis_no)
 
 
 def gathered_by_axis(shard, axes, dim):
@@ -119,9 +126,7 @@
     )
     output_rows = w_out[0]
     branch = jnp.dot(
-        lax.all_gather(attended, HEAD, axis=1, tiled=True),
-        output_rows,
-        preferred_element_type=jnp.float32,
+        _return_all_floor(attended, 1), output_rows, preferred_element_type=jnp.float32
     )
     own_columns = jnp.take(tokens, row_index, axis=0).astype(jnp.float32)
     updated = (own_columns + gate_value[:, None] * branch).astype(jnp.bfloat16)

time: 153 us -> 166 us (1.085)
  waiting for transfers between devices: 74.2 us -> 81.2 us
  starting transfers between devices: 3.44 us -> 8.72 us
    all_to_all x0 -> x1, waiting for transfers between devices: none -> 48.5 us  [_return_all_floor(): plain = jax.lax.all_to_all(step_out, HEAD, 0, 0)]
    all_gather x1 -> x0, waiting for transfers between devices: 41.6 us -> none  [body(): lax.all_gather(attended, HEAD, axis=1, tiled=True)]
    all_to_all x0 -> x1, starting transfers between devices: none -> 5.34 us  [_return_all_floor(): plain = jax.lax.all_to_all(step_out, HEAD, 0, 0)]
  transfers between devices with their start and end apart: 3 -> 3, of which waited for: 3 -> 3; matrix products, arithmetic and copies ran while one was open for 21% -> 19% of each run, Pallas kernels for 0% -> 0%
where the time goes in v1:
time: 166 us; the launch traced here: 165 us
  waiting for transfers between devices  81.2 us (49%)
  local copies, waits for them, and re-layouts  37.6 us (23%)
  matrix products  15.1 us (9%)
  between operations  13.7 us (8%)
  starting transfers between devices  8.72 us (5%)
  other arithmetic  6.82 us (4%)
  blocking collectives  2.13 us (1%)
    all_to_all x1, waiting for transfers between devices, _return_all_floor(): plain = jax.lax.all_to_all(step_out, HEAD, 0, 0)  48.5 us
    all_gather x1, waiting for transfers between devices, gathered_by_axis(): nearer = lax.all_gather(shard, axes[-1], axis=dim, tiled=True)  23.6 us
    another operation x2, local copies, waits for them, and re-layouts, attend_local(): cache_v.reshape(-1, BLOCK, head_count, head_width)[picks]  10 us
    ppermute x1, waiting for transfers between devices, shifted_2(): return lax.ppermute(shard, axis, pairs)  9 us
    another operation x2, local copies, waits for them, and re-layouts, attend_local(): cache_k.reshape(-1, BLOCK, head_count, head_width)[picks]  6.87 us
    all_to_all x1, starting transfers between devices, _return_all_floor(): plain = jax.lax.all_to_all(step_out, HEAD, 0, 0)  5.34 us
    gather x2, local copies, waits for them, and re-layouts, attend_local(): cache_v.reshape(-1, BLOCK, head_count, head_width)[picks]  5.11 us
    gather x2, local copies, waits for them, and re-layouts, attend_local(): cache_k.reshape(-1, BLOCK, head_count, head_width)[picks]  5.07 us
  transfers between devices with their start and end apart: 3, of which 3 were waited for; matrix products, arithmetic and copies ran while one was open for 19% of the time, Pallas kernels for 0%

profile of v1, /device:TPU:2, one launch (start us, length us, event | category | flops | bytes accessed | tf_op | source)
XLA Modules:
  0.0 165.2 jit_solution(15996362019660396736)
XLA Ops:
  6.5 0.0 copy-start
  6.5 0.0 copy-start.10
  6.5 0.0 copy-start.4
  6.5 0.0 all-gather.2.cloned.1.call-start
  6.5 1.1 copy.66
  7.6 0.8 compare_and_fusion
  8.4 1.3 gather_fusion.2
  9.7 0.1 broadcast_select_fusion.1
  9.9 2.1 %all_gather.6 = bf16[512,256]{1,0:T(8,128)(2,1)} all-gather(bf16[512,128]{1,0:T(8,128)(2,1)S(1)} %broadcast_select_fusion.1), channel_id=1, replica_groups=mesh['sec'=32,'head_0'=8,'head_1'=2] {'head_1'}, dimensions={1}, use_global_device_ids=true | all-gather | bytes 393216 | tf_op jit(solution)/shard_map/all_gather | solution.py:23
  12.0 0.0 all-gather.2.cloned.1.call-update
  12.0 0.0 copy-done.10
  12.1 0.1 reshape.185
  12.1 0.0 copy-done.4
  12.1 1.8 %reshape.218 = bf16[32,128,2,64]{3,2,1,0:T(2,128)(2,1)} reshape(bf16[1,4096,128]{2,1,0:T(8,128)(2,1)S(1)} %copy-done.4) | data formatting | bytes 2097152 | tf_op jit(solution)/shard_map/reshape;squeeze | solution.py:37
  14.0 5.0 %copy.38 = bf16[32,128,2,64]{1,3,2,0:T(8,128)(2,1)S(1)} copy(bf16[32,128,2,64]{3,2,1,0:T(2,128)(2,1)} %reshape.218) | data formatting | bytes 2097152 | tf_op jit(solution)/shard_map/reshape;squeeze | solution.py:37
  19.0 2.1 %gather_fusion.1 = bf16[64,128,2,64]{1,3,2,0:T(8,128)(2,1)} fusion(bf16[32,128,2,64]{1,3,2,0:T(8,128)(2,1)S(1)} %copy.38, s32[1024]{0:T(1024)S(1)} %pad_clamp_fusion), kind=kCustom, calls=%fused_computation.2 | custom fusion | bytes 4194560 | tf_op jit(solution)/shard_map/gather | solution.py:37
  21.2 2.9 %copy.39 = bf16[64,128,2,64]{1,0,3,2:T(8,128)(2,1)S(1)} copy(bf16[64,128,2,64]{1,3,2,0:T(8,128)(2,1)} %gather_fusion.1) | data formatting | bytes 4194304 | tf_op jit(solution)/shard_map/gather | solution.py:37
  24.1 2.0 %reshape.166 = bf16[4,2048,2,64]{1,0,3,2:T(4,128)(2,1)} reshape(bf16[64,128,2,64]{1,0,3,2:T(8,128)(2,1)S(1)} %copy.39) | data formatting | bytes 4194304 | tf_op jit(solution)/shard_map/reshape | solution.py:37
  26.2 5.0 %reshape.217 = bf16[32,128,2,64]{3,2,1,0:T(2,128)(2,1)} reshape(bf16[1,4096,128]{2,1,0:T(8,128)(2,1)} %param.25) | data formatting | bytes 2097152 | tf_op jit(solution)/shard_map/reshape;squeeze | solution.py:40
  31.1 5.1 %copy.35 = bf16[32,128,2,64]{1,3,2,0:T(8,128)(2,1)S(1)} copy(bf16[32,128,2,64]{3,2,1,0:T(2,128)(2,1)} %reshape.217) | data formatting | bytes 2097152 | tf_op jit(solution)/shard_map/reshape;squeeze | solution.py:40
  36.2 2.1 %gather_fusion = bf16[64,128,2,64]{1,3,2,0:T(8,128)(2,1)} fusion(bf16[32,128,2,64]{1,3,2,0:T(8,128)(2,1)S(1)} %copy.35, s32[1024]{0:T(1024)S(1)} %pad_clamp_fusion), kind=kCustom, calls=%fused_computation.1 | custom fusion | bytes 4194560 | tf_op jit(solution)/shard_map/gather | solution.py:40
  38.3 3.0 %copy.36 = bf16[64,128,2,64]{1,0,3,2:T(8,128)(2,1)S(1)} copy(bf16[64,128,2,64]{1,3,2,0:T(8,128)(2,1)} %gather_fusion) | data formatting | bytes 4194304 | tf_op jit(solution)/shard_map/gather | solution.py:40
  41.3 2.1 %reshape.165 = bf16[4,2048,2,64]{1,0,3,2:T(4,128)(2,1)} reshape(bf16[64,128,2,64]{1,0,3,2:T(8,128)(2,1)S(1)} %copy.36) | data formatting | bytes 4194304 | tf_op jit(solution)/shard_map/reshape | solution.py:40
  43.4 0.0 copy-start.7
  43.4 0.2 broadcast_compare_fusion
  43.6 23.6 %all-gather.2.cloned.1.call-done = bf16[512,2048]{1,0:T(8,128)(2,1)} async-done(((bf16[512,256]{1,0:T(8,128)(2,1)}), bf16[512,2048]{1,0:T(8,128)(2,1)}) %all-gather.2.cloned.1.call-update) | async-done | bytes 2097168 | tf_op jit(solution)/shard_map/all_gather | solution.py:23
  67.2 0.0 copy-start.3
  67.2 2.2 %fusion.2 = f32[512]{0:T(512)S(1)} fusion(bf16[512,2048]{1,0:T(8,128)(2,1)} %all-gather.2.cloned.1.call-done), kind=kLoop, calls=%fused_computation.10 | loop fusion | flops 3145216 | bytes 2099200 | tf_op jit(solution)/shard_map/reduce_sum | solution.py:103
  69.5 0.0 copy-done.7
  69.5 0.0 copy-done.3
  69.5 0.5 fusion.4
  70.0 0.0 copy-done
  70.0 0.8 convolution_convert_fusion.2
  70.9 0.0 copy-start.2
  70.9 2.0 %convolution_convert_fusion.1 = bf16[512,128]{0,1:T(8,128)(2,1)S(1)} fusion(bf16[512,2048]{1,0:T(8,128)(2,1)S(1)} %fusion.4, bf16[1,2048,128]{2,1,0:T(8,128)(2,1)} %param.21), kind=kOutput, calls=%fused_computation.32 | convolution fusion | flops 268500992 | bytes 2752512 | tf_op jit(solution)/shard_map/dot_general | solution.py:115
  72.9 0.0 copy-done.2
  73.0 3.4 %multiply_reduce_fusion = (f32[4,2,128]{2,1,0:T(2,128)S(1)}, f32[4,2,128,2048]{3,2,1,0:T(8,128)S(1)}) fusion(bf16[4,2048,2,64]{1,0,3,2:T(4,128)(2,1)S(1)} %copy-done.2, bf16[4,128,2,64]{1,0,3,2:T(4,128)(2,1)S(1)} %reshape_reshape.3), kind=kOutput, calls=%fused_computation.5 | convolution fusion | flops 272628736 | bytes 10620928 | tf_op jit(solution)/shard_map/crhd,ckhd->chrk/dot_general | solution.py:45
  76.3 0.0 copy-start.5
  76.3 0.6 fusion.12
  77.0 0.4 copy-done.5
  77.4 0.8 convolution_convert_fusion
  78.2 0.0 copy-start.1
  78.2 1.6 fusion
  79.9 0.0 copy-done.1
  79.9 3.6 %fusion.18 = f32[4,2,8,8,128]{4,3,2,1,0:T(8,128)S(1)} fusion(f32[4,2,128,2048]{3,2,1,0:T(8,128)S(1)} %get-tuple-element.11, f32[4,2,128]{2,1,0:T(2,128)S(1)} %fusion.37, bf16[4,2048,2,64]{1,0,3,2:T(4,128)(2,1)S(1)} %copy-done.1), kind=kOutput, calls=%fused_computation.29 | convolution fusion | flops 274726912 | bytes 10752000 | tf_op jit(solution)/shard_map/chrk,ckhd->crhd/dot_general | solution.py:65
  83.5 0.5 fusion.13
  84.0 0.7 fusion.24
  84.7 1.5 stack.3
  86.2 0.0 copy-start.9
  86.2 0.0 copy-start.8
  86.3 5.3 %all-to-all-start = ((bf16[16,512,128]{1,2,0:T(8,128)(2,1)}), bf16[16,512,128]{1,2,0:T(8,128)(2,1)}, u32[]{:S(2)}, u32[]{:S(2)}) async-start(bf16[16,512,128]{1,2,0:T(8,128)(2,1)} %stack.3), calls=%async_computation | async-start | bytes 4194304 | tf_op jit(solution)/shard_map/all_to_all | solution.py:16
  91.6 0.1 add.84
  91.7 0.0 copy-done.9
  91.7 0.0 copy-done.8
  91.7 0.6 fusion.34
  92.3 48.5 %all-to-all-done = bf16[16,512,128]{1,2,0:T(8,128)(2,1)} async-done(((bf16[16,512,128]{1,2,0:T(8,128)(2,1)}), bf16[16,512,128]{1,2,0:T(8,128)(2,1)}, u32[]{:S(2)}, u32[]{:S(2)}) %all-to-all-start) | async-done | bytes 2097184 | tf_op jit(solution)/shard_map/all_to_all | solution.py:16
  140.8 0.0 copy-start.6
  140.8 2.5 %fusion.23 = bf16[512,128]{1,0:T(8,128)(2,1)S(1)} fusion(bf16[512,2048]{0,1:T(8,128)(2,1)} %bitcast.25, bf16[1,2048,128]{2,1,0:T(8,128)(2,1)} %param.23, bf16[512,128]{1,0:T(8,128)(2,1)S(1)} %broadcast_select_fusion.1, f32[512]{0:T(512)S(1)} %add_divide_fusion), kind=kOutput, calls=%fused_computation.30 | convolution fusion | flops 268697600 | bytes 2885632 | tf_op jit(solution)/shard_map/dot_general | solution.py:128
  143.3 1.9 %scatter_fusion = bf16[1024,128]{1,0:T(8,128)(2,1)S(1)} fusion(bf16[1024,128]{1,0:T(8,128)(2,1)S(1)} %copy.66, s32[512]{0:T(512)S(1)} %bitcast.93, bf16[512,128]{1,0:T(8,128)(2,1)S(1)} %fusion.23), kind=kCustom, calls=%fused_computation.3 | custom fusion | bytes 395264 | tf_op jit(solution)/shard_map/scatter | solution.py:133
  145.2 3.4 %collective-permute-start = (bf16[1024,128]{1,0:T(8,128)(2,1)S(1)}, bf16[1024,128]{1,0:T(8,128)(2,1)S(1)}, u32[]{:S(2)}, u32[]{:S(2)}) collective-permute-start(bf16[1024,128]{1,0:T(8,128)(2,1)S(1)} %scatter_fusion), channel_id=1, source_target_pairs={{0,16},{16,32},{32,48},{48,64},{64,80},{80,96},{96,112},{112,128},... | collective-permute-start | bytes 786440 | tf_op jit(solution)/shard_map/ppermute | solution.py:30
  148.6 9.0 %collective-permute-done = bf16[1024,128]{1,0:T(8,128)(2,1)S(1)} collective-permute-done((bf16[1024,128]{1,0:T(8,128)(2,1)S(1)}, bf16[1024,128]{1,0:T(8,128)(2,1)S(1)}, u32[]{:S(2)}, u32[]{:S(2)}) %collective-permute-start) | collective-permute-done | bytes 262176 | tf_op jit(solution)/shard_map/ppermute | solution.py:30
  157.6 0.0 copy-done.6
  157.6 0.7 broadcast_select_fusion
  (12 shorter events, 0.1 us)
Async XLA Ops:
  6.5 63.5 %copy-start = (bf16[1,2048,128]{2,1,0:T(8,128)(2,1)S(1)}, bf16[1,2048,128]{2,1,0:T(8,128)(2,1)}, u32[]{:S(2)}) copy-start(bf16[1,2048,128]{2,1,0:T(8,128)(2,1)} %param.20) | copy-start | bytes 1572868
  6.5 5.5 %copy-start.10 = (s32[1,4,16]{2,1,0:T(4,128)S(1)}, s32[1,4,16]{2,1,0:T(4,128)}, u32[]{:S(2)}) copy-start(s32[1,4,16]{2,1,0:T(4,128)} %param.17) | copy-start | bytes 772
  6.5 5.6 %copy-start.4 = (bf16[1,4096,128]{2,1,0:T(8,128)(2,1)S(1)}, bf16[1,4096,128]{2,1,0:T(8,128)(2,1)}, u32[]{:S(2)}) copy-start(bf16[1,4096,128]{2,1,0:T(8,128)(2,1)} %param.24) | copy-start | bytes 3145732
  6.5 60.7 %all-gather.2.cloned.1.call-start = ((), (), s32[]{:S(2)}) async-start(), calls=%async_computation.1 | async-start | bytes 2359296 | tf_op jit(solution)/shard_map/all_gather | solution.py:23
  43.4 26.1 %copy-start.7 = (f32[1,2048]{1,0:T(1,128)S(1)}, f32[1,2048]{1,0:T(1,128)}, u32[]{:S(2)}) copy-start(f32[1,2048]{1,0:T(1,128)} %param.18) | copy-start | bytes 24580
  67.2 2.2 %copy-start.3 = (bf16[512,2048]{1,0:T(8,128)(2,1)S(1)}, bf16[512,2048]{1,0:T(8,128)(2,1)}, u32[]{:S(2)}) copy-start(bf16[512,2048]{1,0:T(8,128)(2,1)} %all-gather.2.cloned.1.call-done) | copy-start | bytes 6291460
  70.9 2.0 %copy-start.2 = (bf16[4,2048,2,64]{1,0,3,2:T(4,128)(2,1)S(1)}, bf16[4,2048,2,64]{1,0,3,2:T(4,128)(2,1)}, u32[]{:S(2)}) copy-start(bf16[4,2048,2,64]{1,0,3,2:T(4,128)(2,1)} %reshape.166) | copy-start | bytes 6291460
  76.3 1.0 copy-start.5
  78.2 1.7 %copy-start.1 = (bf16[4,2048,2,64]{1,0,3,2:T(4,128)(2,1)S(1)}, bf16[4,2048,2,64]{1,0,3,2:T(4,128)(2,1)}, u32[]{:S(2)}) copy-start(bf16[4,2048,2,64]{1,0,3,2:T(4,128)(2,1)} %reshape.165) | copy-start | bytes 6291460
  86.2 5.4 %copy-start.9 = (s32[1,4,128]{2,1,0:T(4,128)S(1)}, s32[1,4,128]{2,1,0:T(4,128)}, u32[]{:S(2)}) copy-start(s32[1,4,128]{2,1,0:T(4,128)} %param.16) | copy-start | bytes 6148
  86.2 5.4 %copy-start.8 = (bf16[1,2048]{1,0:T(2,128)(2,1)S(1)}, bf16[1,2048]{1,0:T(2,128)(2,1)}, u32[]{:S(2)}) copy-start(bf16[1,2048]{1,0:T(2,128)(2,1)} %param.19) | copy-start | bytes 12292
  86.3 54.6 %all-to-all-start = ((bf16[16,512,128]{1,2,0:T(8,128)(2,1)}), bf16[16,512,128]{1,2,0:T(8,128)(2,1)}, u32[]{:S(2)}, u32[]{:S(2)}) async-start(bf16[16,512,128]{1,2,0:T(8,128)(2,1)} %stack.3), calls=%async_computation | async-start | bytes 4194304 | tf_op jit(solution)/shard_map/all_to_all | solution.py:16
  140.8 16.8 %copy-start.6 = (bf16[1024,128]{1,0:T(8,128)(2,1)S(1)}, bf16[1024,128]{1,0:T(8,128)(2,1)}, u32[]{:S(2)}) copy-start(bf16[1024,128]{1,0:T(8,128)(2,1)} %param.15) | copy-start | bytes 786436
  145.2 12.4 %collective-permute-start = (bf16[1024,128]{1,0:T(8,128)(2,1)S(1)}, bf16[1024,128]{1,0:T(8,128)(2,1)S(1)}, u32[]{:S(2)}, u32[]{:S(2)}) collective-permute-start(bf16[1024,128]{1,0:T(8,128)(2,1)S(1)} %scatter_fusion), channel_id=1, source_target_pairs={{0,16},{16,32},{32,48},{48,64},{64,80},{80,96},{96,112},{112,128},... | collective-permute-start | bytes 786440 | tf_op jit(solution)/shard_map/ppermute | solution.py:30
Sparse Core Ops, SparseCore 0:
  12.2 55.0 all-gather.1
